TPU v7x, 32 devices: a whole 2x2x4 slice. The times are simulated.
32 devices in a mesh: dp: 8 (over z, x), fsdp: 4 (over y, core).
Axes of the slice: x: 2, y: 2, z: 4, core: 2. Of those that a mesh axis runs over, the one named last changes fastest.
Arguments:
- tokens: bfloat16 [16384, 960], P(('dp', 'fsdp')), may hold values from -6 to 6
- norm_gains: bfloat16 [2, 960], P(None, 'dp'), may hold values from 0.5 to 1.5
- query_weight: bfloat16 [960, 960], P('fsdp', 'dp'), may hold values from -0.1875 to 0.1875
- key_weight: bfloat16 [960, 320], P('fsdp', 'dp'), may hold values from -0.1875 to 0.1875
- value_weight: bfloat16 [960, 320], P('fsdp', 'dp'), may hold values from -0.1875 to 0.1875
- out_weight: bfloat16 [960, 960], P('fsdp', 'dp'), may hold values from -6 to 6
- gate_weight: bfloat16 [960, 2560], P('fsdp', 'dp'), may hold values from -0.1875 to 0.1875
- up_weight: bfloat16 [960, 2560], P('fsdp', 'dp'), may hold values from -0.1875 to 0.1875
- down_weight: bfloat16 [2560, 960], P('fsdp', 'dp'), may hold values from -0.125 to 0.125
- segment_ids: int32 [16384], P('dp'), may hold values from 0 to 2, as said below
- out_grad: bfloat16 [16384, 960], P(('dp', 'fsdp')), may hold values from -6 to 6
Outputs:
- output: bfloat16 [16384, 960], P(('dp', 'fsdp'))
- input_grad: float32 [16384, 960], P(('dp', 'fsdp'))
- gains_grad: float32 [2, 960], P(None, 'dp')
- query_grad: float32 [960, 960], P('fsdp', 'dp')
- key_grad: float32 [960, 320], P('fsdp', 'dp')
- value_grad: float32 [960, 320], P('fsdp', 'dp')
- out_weight_grad: float32 [960, 960], P('fsdp', 'dp')
- gate_grad: float32 [960, 2560], P('fsdp', 'dp')
- up_grad: float32 [960, 2560], P('fsdp', 'dp')
- down_grad: float32 [2560, 960], P('fsdp', 'dp')
Inputs may be any that keep to these rules, and one draw needn't show every extreme that they name: `segment_ids`: each block of 2048 tokens (the tokens of one dp index) holds three sequences with ids 0, 1 and 2 in this order, each nonempty. Rows are counted from 0 within the block: the first row of sequence 1 lies in rows 1 to 256, and its last row lies in rows 1791 to 2046.
All inputs are finite; a program needn't handle non-finite values.
Results may differ from a plain program's by a relative error of at most 0.012.
Values may be sent and summed in bfloat16 or wider, within the bound.
No kernel may reach another device: no remote copies, remote signals or barrier semaphores. Data moves between devices by JAX's collectives and lax.ppermute only.
A program may use at most 128 MiB of HBM per device.

v0:
```python
import math

import jax
import jax.numpy as jnp
from jax import lax
from jax.sharding import PartitionSpec as P

D = 960
HEADS = 15
KV_HEADS = 5
HEAD_DIM = 64
KV_WIDTH = 320


norm_eps = 1e-05
masked_value = -1e30


def outer_sum(operand, other):
    return lax.dot_general(
        operand, other, (((0,), (0,)), ((), ())), preferred_element_type=jnp.float32
    )


def times_back(operand, weight):
    return lax.dot_general(
        operand, weight, (((1,), (1,)), ((), ())), preferred_element_type=jnp.float32
    )


def rope_tables(positions):
    half_dim = HEAD_DIM // 2
    frequency = jnp.exp(
        jnp.arange(half_dim, dtype=jnp.float32) * (-2.0 * math.log(10000.0) / HEAD_DIM)
    )
    angles = positions.astype(jnp.float32)[:, None] * frequency[None, :]
    return (jnp.cos(angles)[:, None, :], jnp.sin(angles)[:, None, :])


def rotate(values, cosine, sine):
    half_dim = values.shape[-1] // 2
    first_half = values[..., :half_dim]
    second = values[..., half_dim:]
    return jnp.concatenate(
        [first_half * cosine - second * sine, second * cosine + first_half * sine], axis=-1
    )


def rotate_back(gradient, cosine, sine):
    half_dim = gradient.shape[-1] // 2
    first_half = gradient[..., :half_dim]
    second = gradient[..., half_dim:]
    return jnp.concatenate(
        [first_half * cosine + second * sine, second * cosine - first_half * sine], axis=-1
    )


def gather_weights(
    query_weight,
    key_weight,
    value_weight,
    out_weight,
    gate_weight,
    up_weight,
    down_weight,
    norm_gains,
):
    row_parts = (
        lax.all_gather(query_weight, "fsdp", axis=0, tiled=True),
        lax.all_gather(key_weight, "fsdp", axis=0, tiled=True),
        lax.all_gather(value_weight, "fsdp", axis=0, tiled=True),
        lax.all_gather(out_weight, "fsdp", axis=0, tiled=True),
        lax.all_gather(gate_weight, "fsdp", axis=0, tiled=True),
        lax.all_gather(up_weight, "fsdp", axis=0, tiled=True),
        lax.all_gather(down_weight, "fsdp", axis=0, tiled=True),
    )
    gathered = (
        lax.all_gather(row_parts[0], "dp", axis=1, tiled=True),
        lax.all_gather(row_parts[1], "dp", axis=1, tiled=True),
        lax.all_gather(row_parts[2], "dp", axis=1, tiled=True),
        lax.all_gather(row_parts[3], "dp", axis=1, tiled=True),
        lax.all_gather(row_parts[4], "dp", axis=1, tiled=True),
        lax.all_gather(row_parts[5], "dp", axis=1, tiled=True),
        lax.all_gather(row_parts[6], "dp", axis=1, tiled=True),
        lax.all_gather(norm_gains, "dp", axis=1, tiled=True),
    )
    return gathered


def reduce_grads(
    query_term, key_term, value_term, out_term, gate_term, up_term, down_term, gains_term
):
    column_sums = (
        lax.psum_scatter(query_term, "dp", scatter_dimension=1, tiled=True),
        lax.psum_scatter(key_term, "dp", scatter_dimension=1, tiled=True),
        lax.psum_scatter(value_term, "dp", scatter_dimension=1, tiled=True),
        lax.psum_scatter(out_term, "dp", scatter_dimension=1, tiled=True),
        lax.psum_scatter(gate_term, "dp", scatter_dimension=1, tiled=True),
        lax.psum_scatter(up_term, "dp", scatter_dimension=1, tiled=True),
        lax.psum_scatter(down_term, "dp", scatter_dimension=1, tiled=True),
        lax.psum_scatter(gains_term, "dp", scatter_dimension=1, tiled=True),
    )
    row_sums = (
        lax.psum_scatter(column_sums[0], "fsdp", scatter_dimension=0, tiled=True),
        lax.psum_scatter(column_sums[1], "fsdp", scatter_dimension=0, tiled=True),
        lax.psum_scatter(column_sums[2], "fsdp", scatter_dimension=0, tiled=True),
        lax.psum_scatter(column_sums[3], "fsdp", scatter_dimension=0, tiled=True),
        lax.psum_scatter(column_sums[4], "fsdp", scatter_dimension=0, tiled=True),
        lax.psum_scatter(column_sums[5], "fsdp", scatter_dimension=0, tiled=True),
        lax.psum_scatter(column_sums[6], "fsdp", scatter_dimension=0, tiled=True),
    )
    gains_part = column_sums[7]
    gains_total = lax.psum(gains_part, "fsdp")
    return tuple(row_sums) + (gains_total,)


def per_device(
    tokens,
    norm_gains,
    query_weight,
    key_weight,
    value_weight,
    out_weight,
    gate_weight,
    up_weight,
    down_weight,
    segment_ids,
    out_grad,
):
    tok_rows = tokens.shape[0]
    group_rows = segment_ids.shape[0]
    ratio_heads = HEADS // KV_HEADS
    first_row = lax.axis_index("fsdp") * tok_rows
    w_query, w_key, w_value, w_out, w_gate, w_up, w_down, gains_full = gather_weights(
        query_weight,
        key_weight,
        value_weight,
        out_weight,
        gate_weight,
        up_weight,
        down_weight,
        norm_gains,
    )
    local_ids = lax.dynamic_slice_in_dim(segment_ids, first_row, tok_rows)
    global_rows = first_row + jnp.arange(tok_rows, dtype=jnp.int32)
    earlier = jnp.sum((segment_ids[None, :] < local_ids[:, None]).astype(jnp.int32), axis=1)
    positions = global_rows - earlier
    allowed = (segment_ids[None, :] == local_ids[:, None]) & (
        jnp.arange(group_rows, dtype=jnp.int32)[None, :] <= global_rows[:, None]
    )
    cosine, sine = rope_tables(positions)
    inputs = tokens.astype(jnp.float32)
    gain_one = gains_full[0].astype(jnp.float32)
    gain_two = gains_full[1].astype(jnp.float32)
    inv_one = lax.rsqrt(jnp.mean(inputs * inputs, axis=1, keepdims=True) + norm_eps)
    normed = (inputs * inv_one * gain_one).astype(jnp.bfloat16)
    query_raw = jnp.dot(normed, w_query, preferred_element_type=jnp.float32).reshape(
        tok_rows, HEADS, HEAD_DIM
    )
    key_raw = jnp.dot(normed, w_key, preferred_element_type=jnp.float32).reshape(
        tok_rows, KV_HEADS, HEAD_DIM
    )
    value_low = jnp.dot(normed, w_value, preferred_element_type=jnp.float32).astype(jnp.bfloat16)
    query_heads = rotate(query_raw, cosine, sine).astype(jnp.bfloat16)
    key_low = rotate(key_raw, cosine, sine).astype(jnp.bfloat16).reshape(tok_rows, KV_WIDTH)
    key_all, value_all = (
        lax.all_gather(key_low, "fsdp", axis=0, tiled=True),
        lax.all_gather(value_low, "fsdp", axis=0, tiled=True),
    )
    key_heads = key_all.reshape(group_rows, KV_HEADS, HEAD_DIM)
    value_heads = value_all.reshape(group_rows, KV_HEADS, HEAD_DIM)

    def head_scores(query_one, key_one):
        scores = (
            jnp.einsum("qd,kd->qk", query_one, key_one, preferred_element_type=jnp.float32) * 0.125
        )
        return jnp.where(allowed, scores, masked_value)

    def forward_head(head_index, loop_state):
        attended_acc, totals_acc = loop_state
        query_one = lax.dynamic_index_in_dim(query_heads, head_index, 1, keepdims=False)
        key_one = lax.dynamic_index_in_dim(key_heads, head_index // ratio_heads, 1, keepdims=False)
        value_one = lax.dynamic_index_in_dim(
            value_heads, head_index // ratio_heads, 1, keepdims=False
        )
        masked = head_scores(query_one, key_one)
        row_max = jnp.max(masked, axis=1, keepdims=True)
        log_total = row_max + jnp.log(jnp.sum(jnp.exp(masked - row_max), axis=1, keepdims=True))
        soft_probs = jnp.exp(masked - log_total).astype(jnp.bfloat16)
        result = jnp.dot(soft_probs, value_one, preferred_element_type=jnp.float32).astype(
            jnp.bfloat16
        )
        attended_acc = lax.dynamic_update_index_in_dim(attended_acc, result, head_index, 1)
        totals_acc = lax.dynamic_update_index_in_dim(totals_acc, log_total[:, 0], head_index, 1)
        return (attended_acc, totals_acc)

    attended_heads, totals = lax.fori_loop(
        0,
        HEADS,
        forward_head,
        (
            jnp.zeros((tok_rows, HEADS, HEAD_DIM), jnp.bfloat16),
            jnp.zeros((tok_rows, HEADS), jnp.float32),
        ),
    )
    attended = attended_heads.reshape(tok_rows, D)
    hidden = inputs + jnp.dot(attended, w_out, preferred_element_type=jnp.float32)
    inv_two = lax.rsqrt(jnp.mean(hidden * hidden, axis=1, keepdims=True) + norm_eps)
    normed_two = (hidden * inv_two * gain_two).astype(jnp.bfloat16)
    gate_act = jnp.dot(normed_two, w_gate, preferred_element_type=jnp.float32)
    up_act = jnp.dot(normed_two, w_up, preferred_element_type=jnp.float32)
    sigmoid = jax.nn.sigmoid(gate_act)
    mixed = (gate_act * sigmoid * up_act).astype(jnp.bfloat16)
    output = hidden + jnp.dot(mixed, w_down, preferred_element_type=jnp.float32)
    w_query, w_key, w_value, w_out, w_gate, w_up, w_down, gains_full = gather_weights(
        query_weight,
        key_weight,
        value_weight,
        out_weight,
        gate_weight,
        up_weight,
        down_weight,
        norm_gains,
    )
    grad_output = out_grad.astype(jnp.float32)
    grad_w_down = outer_sum(mixed, out_grad)
    grad_mixed = times_back(out_grad, w_down)
    grad_gate = (grad_mixed * up_act * sigmoid * (1.0 + gate_act * (1.0 - sigmoid))).astype(
        jnp.bfloat16
    )
    grad_up = (grad_mixed * gate_act * sigmoid).astype(jnp.bfloat16)
    grad_w_gate = outer_sum(normed_two, grad_gate)
    grad_w_up = outer_sum(normed_two, grad_up)
    grad_normed_two = times_back(grad_gate, w_gate) + times_back(grad_up, w_up)
    weighted_two = grad_normed_two * gain_two
    grad_gain_two = jnp.sum(grad_normed_two * hidden * inv_two, axis=0)
    grad_hidden = (
        grad_output
        + inv_two * weighted_two
        - hidden
        * (inv_two * inv_two * inv_two)
        * jnp.mean(weighted_two * hidden, axis=1, keepdims=True)
    )
    branch_grad = grad_hidden.astype(jnp.bfloat16)
    grad_w_out = outer_sum(attended, branch_grad)
    grad_heads = (
        times_back(branch_grad, w_out).astype(jnp.bfloat16).reshape(tok_rows, HEADS, HEAD_DIM)
    )

    def backward_head(head_index, loop_state):
        query_acc, key_acc, value_acc = loop_state
        kv_index = head_index // ratio_heads
        query_one = lax.dynamic_index_in_dim(query_heads, head_index, 1, keepdims=False)
        key_one = lax.dynamic_index_in_dim(key_heads, kv_index, 1, keepdims=False)
        value_one = lax.dynamic_index_in_dim(value_heads, kv_index, 1, keepdims=False)
        grad_one = lax.dynamic_index_in_dim(grad_heads, head_index, 1, keepdims=False)
        log_total = lax.dynamic_index_in_dim(totals, head_index, 1, keepdims=True)
        soft_probs = jnp.exp(head_scores(query_one, key_one) - log_total)
        grad_probs = jnp.einsum(
            "qd,kd->qk", grad_one, value_one, preferred_element_type=jnp.float32
        )
        row_dot = jnp.sum(soft_probs * grad_probs, axis=1, keepdims=True)
        grad_scores = (soft_probs * (grad_probs - row_dot)).astype(jnp.bfloat16)
        query_term = jnp.dot(grad_scores, key_one, preferred_element_type=jnp.float32) * 0.125
        key_term = outer_sum(grad_scores, query_one) * 0.125
        value_term = outer_sum(soft_probs.astype(jnp.bfloat16), grad_one)
        query_acc = lax.dynamic_update_index_in_dim(query_acc, query_term, head_index, 1)
        key_acc = lax.dynamic_update_index_in_dim(
            key_acc,
            lax.dynamic_index_in_dim(key_acc, kv_index, 1, keepdims=False) + key_term,
            kv_index,
            1,
        )
        value_acc = lax.dynamic_update_index_in_dim(
            value_acc,
            lax.dynamic_index_in_dim(value_acc, kv_index, 1, keepdims=False) + value_term,
            kv_index,
            1,
        )
        return (query_acc, key_acc, value_acc)

    grad_query_rot, key_grads, value_grads = lax.fori_loop(
        0,
        HEADS,
        backward_head,
        (
            jnp.zeros((tok_rows, HEADS, HEAD_DIM), jnp.float32),
            jnp.zeros((group_rows, KV_HEADS, HEAD_DIM), jnp.float32),
            jnp.zeros((group_rows, KV_HEADS, HEAD_DIM), jnp.float32),
        ),
    )
    key_sum, value_sum = (
        lax.psum_scatter(
            key_grads.reshape(group_rows, KV_WIDTH), "fsdp", scatter_dimension=0, tiled=True
        ),
        lax.psum_scatter(
            value_grads.reshape(group_rows, KV_WIDTH), "fsdp", scatter_dimension=0, tiled=True
        ),
    )
    grad_query_raw = (
        rotate_back(grad_query_rot, cosine, sine).reshape(tok_rows, D).astype(jnp.bfloat16)
    )
    grad_key_raw = (
        rotate_back(key_sum.reshape(tok_rows, KV_HEADS, HEAD_DIM), cosine, sine)
        .reshape(tok_rows, KV_WIDTH)
        .astype(jnp.bfloat16)
    )
    grad_value_raw = value_sum.astype(jnp.bfloat16)
    grad_w_query = outer_sum(normed, grad_query_raw)
    grad_w_key = outer_sum(normed, grad_key_raw)
    grad_w_value = outer_sum(normed, grad_value_raw)
    grad_normed = (
        times_back(grad_query_raw, w_query)
        + times_back(grad_key_raw, w_key)
        + times_back(grad_value_raw, w_value)
    )
    weighted_one = grad_normed * gain_one
    grad_gain_one = jnp.sum(grad_normed * inputs * inv_one, axis=0)
    input_grad = (
        grad_hidden
        + inv_one * weighted_one
        - inputs
        * (inv_one * inv_one * inv_one)
        * jnp.mean(weighted_one * inputs, axis=1, keepdims=True)
    )
    grad_gains = jnp.stack([grad_gain_one, grad_gain_two])
    reduced = reduce_grads(
        grad_w_query,
        grad_w_key,
        grad_w_value,
        grad_w_out,
        grad_w_gate,
        grad_w_up,
        grad_w_down,
        grad_gains,
    )
    return (
        output.astype(jnp.bfloat16),
        input_grad,
        reduced[7],
        reduced[0],
        reduced[1],
        reduced[2],
        reduced[3],
        reduced[4],
        reduced[5],
        reduced[6],
    )


def solution(mesh):
    placed = (
        P(("dp", "fsdp"), None),
        P(None, "dp"),
        P("fsdp", "dp"),
        P("fsdp", "dp"),
        P("fsdp", "dp"),
        P("fsdp", "dp"),
        P("fsdp", "dp"),
        P("fsdp", "dp"),
        P("fsdp", "dp"),
        P("dp"),
        P(("dp", "fsdp"), None),
    )
    return jax.shard_map(
        per_device,
        mesh=mesh,
        in_specs=placed,
        out_specs=(
            P(("dp", "fsdp"), None),
            P(("dp", "fsdp"), None),
            P(None, "dp"),
            P("fsdp", "dp"),
            P("fsdp", "dp"),
            P("fsdp", "dp"),
            P("fsdp", "dp"),
            P("fsdp", "dp"),
            P("fsdp", "dp"),
            P("fsdp", "dp"),
        ),
        check_vma=False,
    )
```

profile of v0, /device:TPU:0, one launch (start us, length us, event | category | flops | bytes accessed | tf_op | source)
XLA Modules:
  0.0 1776.3 jit_solution(3399977218010492315)
XLA Ops:
  15.6 20.9 %all-gather = bf16[8,120,2]{1,2,0:T(2,128)(2,1)S(1)} all-gather(bf16[1,120,2]{1,2,0:T(2,128)(2,1)} %bitcast.214), channel_id=1, replica_groups=mesh['dp'=8,'fsdp'=4] {'dp'}, dimensions={0}, use_global_device_ids=true | all-gather | bytes 4320 | tf_op jit(solution)/shard_map/all_gather | solution.py:85
  45.5 33.0 %all_gather.69 = bf16[960,320]{0,1:T(8,128)(2,1)S(1)} all-gather(bf16[960,40]{0,1:T(8,128)(2,1)S(1)} %reshape.198), channel_id=1, replica_groups=mesh['dp'=8,'fsdp'=4] {'dp'}, dimensions={1}, use_global_device_ids=true | all-gather | bytes 691200 | tf_op jit(solution)/shard_map/all_gather | solution.py:79
  85.7 31.9 %all_gather.72 = bf16[960,320]{0,1:T(8,128)(2,1)S(1)} all-gather(bf16[960,40]{0,1:T(8,128)(2,1)S(1)} %reshape.200), channel_id=1, replica_groups=mesh['dp'=8,'fsdp'=4] {'dp'}, dimensions={1}, use_global_device_ids=true | all-gather | bytes 691200 | tf_op jit(solution)/shard_map/all_gather | solution.py:80
  126.5 11.6 all-gather.3
  162.2 74.9 %while.38 = (s32[]{:T(128)}, bf16[512,15,64]{0,2,1:T(8,128)(2,1)S(1)}, f32[512,15]{0,1:T(8,128)S(1)}, bf16[512,15,64]{0,2,1:T(8,128)(2,1)S(1)}, bf16[2048,5,64]{...) while((s32[]{:T(128)}, ...), condition=%wide.region_5.6_spmd.clone, body=%wide.region_2.5_spmd.clone.sunk | while | flops 278953472 | bytes 13270273 | solution.py:197
  242.8 33.5 %all-gather.21.cloned.1.call-done = bf16[960,2560]{0,1:T(8,128)(2,1)} async-done(((bf16[960,320]{0,1:T(8,128)(2,1)}), bf16[960,2560]{0,1:T(8,128)(2,1)}) %all-gather.21.cloned.1.call-update) | async-done | bytes 4915216 | tf_op jit(solution)/shard_map/all_gather | solution.py:82
  284.4 78.4 %all-gather.23.cloned.1.call-done = bf16[960,2560]{0,1:T(8,128)(2,1)} async-done(((bf16[960,320]{0,1:T(8,128)(2,1)}), bf16[960,2560]{0,1:T(8,128)(2,1)}) %all-gather.23.cloned.1.call-update) | async-done | bytes 4915216 | tf_op jit(solution)/shard_map/all_gather | solution.py:83
  370.8 74.7 %all-gather.25.cloned.1.call-done = bf16[2560,960]{0,1:T(8,128)(2,1)} async-done(((bf16[2560,120]{0,1:T(8,128)(2,1)}), bf16[2560,960]{0,1:T(8,128)(2,1)}) %all-gather.25.cloned.1.call-update) | async-done | bytes 4915216 | tf_op jit(solution)/shard_map/all_gather | solution.py:84
  474.6 196.2 %while.39 = (s32[]{:T(128)}, f32[512,15,64]{0,2,1:T(8,128)}, f32[2048,5,64]{0,2,1:T(8,128)}, f32[2048,5,64]{0,2,1:T(8,128)}, bf16[512,15,64]{0,2,1:T(8,128)(2,1)...) while((s32[]{:T(128)}, f32[512,15,64]{0,2,1:T(8,128)}, ...), condition=%wide.region_10.11_spmd.clone, body=%wide.region_8.10_spmd.clone.sunk | while | flops 684097024 | bytes 36856616 | solution.py:282
  671.8 32.0 %reduce-scatter.30.cloned.1.call-done = f32[512,320]{0,1:T(8,128)} async-done(((f32[2048,320]{0,1:T(8,128)}), f32[512,320]{0,1:T(8,128)}) %reduce-scatter.30.cloned.1.call-update) | async-done | bytes 655376 | tf_op jit(solution)/shard_map/reduce_scatter | solution.py:293
  706.8 34.4 %reduce-scatter.32.cloned.1.call-done = f32[512,320]{0,1:T(8,128)} async-done(((f32[2048,320]{0,1:T(8,128)}), f32[512,320]{0,1:T(8,128)}) %reduce-scatter.32.cloned.1.call-update) | async-done | bytes 655376 | tf_op jit(solution)/shard_map/reduce_scatter | solution.py:296
  781.3 27.6 %reduce-scatter.36.cloned.1.call-done = f32[960,40]{0,1:T(8,128)} async-done(((f32[960,320]{0,1:T(8,128)}), f32[960,40]{0,1:T(8,128)}) %reduce-scatter.36.cloned.1.call-update) | async-done | bytes 153616 | tf_op jit(solution)/shard_map/reduce_scatter | solution.py:95
  810.9 64.8 %reduce-scatter.38.cloned.1.call-done = f32[960,40]{0,1:T(8,128)} async-done(((f32[960,320]{0,1:T(8,128)}), f32[960,40]{0,1:T(8,128)}) %reduce-scatter.38.cloned.1.call-update) | async-done | bytes 153616 | tf_op jit(solution)/shard_map/reduce_scatter | solution.py:96
  877.6 178.4 %reduce-scatter.42.cloned.1.call-done = f32[960,320]{0,1:T(8,128)} async-done(((f32[960,2560]{0,1:T(8,128)}), f32[960,320]{0,1:T(8,128)}) %reduce-scatter.42.cloned.1.call-update) | async-done | bytes 1228816 | tf_op jit(solution)/shard_map/reduce_scatter | solution.py:98
  1059.2 177.6 %reduce-scatter.44.cloned.1.call-done = f32[960,320]{0,1:T(8,128)} async-done(((f32[960,2560]{0,1:T(8,128)}), f32[960,320]{0,1:T(8,128)}) %reduce-scatter.44.cloned.1.call-update) | async-done | bytes 1228816 | tf_op jit(solution)/shard_map/reduce_scatter | solution.py:99
  1239.8 83.9 %reduce-scatter.50.cloned.1.call-done = f32[120,960]{1,0:T(8,128)} async-done(((f32[960,960]{1,0:T(8,128)}), f32[120,960]{1,0:T(8,128)}) %reduce-scatter.50.cloned.1.call-update) | async-done | bytes 460816
  1325.9 85.9 %reduce-scatter.56.cloned.1.call-done = f32[120,960]{1,0:T(8,128)} async-done(((f32[960,960]{1,0:T(8,128)}), f32[120,960]{1,0:T(8,128)}) %reduce-scatter.56.cloned.1.call-update) | async-done | bytes 460816
  1415.2 168.8 %reduce-scatter.46.cloned.1.call-done = f32[2560,120]{0,1:T(8,128)} async-done(((f32[2560,960]{0,1:T(8,128)}), f32[2560,120]{0,1:T(8,128)}) %reduce-scatter.46.cloned.1.call-update) | async-done | bytes 1228816 | tf_op jit(solution)/shard_map/reduce_scatter | solution.py:100
  1597.2 19.7 %all-reduce = f32[2,960]{1,0:T(2,128)S(1)} all-reduce(f32[2,960]{1,0:T(2,128)S(1)} %pad_maximum_fusion.4), channel_id=4, replica_groups=mesh['dp'=8,'fsdp'=4] {'dp'}, use_global_device_ids=true, to_apply=%region_16.17.clone | all-reduce | flops 1920 | bytes 15360
  1632.3 28.5 %reduce-scatter.58.cloned.1.call-done = f32[240,320]{1,0:T(8,128)} async-done(((f32[960,320]{1,0:T(8,128)}), f32[240,320]{1,0:T(8,128)}) %reduce-scatter.58.cloned.1.call-update) | async-done | bytes 307216
  1662.7 28.3 %reduce-scatter.60.cloned.1.call-done = f32[240,320]{1,0:T(8,128)} async-done(((f32[960,320]{1,0:T(8,128)}), f32[240,320]{1,0:T(8,128)}) %reduce-scatter.60.cloned.1.call-update) | async-done | bytes 307216
  1692.9 22.7 %reduce-scatter.34.cloned.1.call-done = f32[240,120]{1,0:T(8,128)} async-done(((f32[960,120]{1,0:T(8,128)}), f32[240,120]{1,0:T(8,128)}) %reduce-scatter.34.cloned.1.call-update) | async-done | bytes 115216 | tf_op jit(solution)/shard_map/reduce_scatter | solution.py:104
  1715.6 24.5 %reduce-scatter.40.cloned.1.call-done = f32[240,120]{1,0:T(8,128)} async-done(((f32[960,120]{1,0:T(8,128)}), f32[240,120]{1,0:T(8,128)}) %reduce-scatter.40.cloned.1.call-update) | async-done | bytes 115216 | tf_op jit(solution)/shard_map/reduce_scatter | solution.py:107
  1740.1 29.2 %reduce-scatter.48.cloned.1.call-done = f32[640,120]{0,1:T(8,128)} async-done(((f32[2560,120]{0,1:T(8,128)}), f32[640,120]{0,1:T(8,128)}) %reduce-scatter.48.cloned.1.call-update) | async-done | bytes 307216 | tf_op jit(solution)/shard_map/reduce_scatter | solution.py:110
  (378 shorter events, 468.6 us)
Async XLA Ops:
  7.2 151.5 %all-gather.13.cloned.1.call-start = ((), (), s32[]{:S(2)}) async-start(), calls=%async_computation.16 | async-start | bytes 2211840 | tf_op jit(solution)/shard_map/all_gather | solution.py:78
  15.6 146.3 %all-gather.15.cloned.1.call-start = ((), (), s32[]{:S(2)}) async-start(), calls=%async_computation.17 | async-start | bytes 1638400 | tf_op jit(solution)/shard_map/all_gather | solution.py:167
  80.2 81.8 %all-gather.17.cloned.1.call-start = ((), (), s32[]{:S(2)}) async-start(), calls=%async_computation.18 | async-start | bytes 1638400 | tf_op jit(solution)/shard_map/all_gather | solution.py:168
  119.8 117.3 %all-gather.19.cloned.1.call-start = ((), (), s32[]{:S(2)}) async-start(), calls=%async_computation.19 | async-start | bytes 2211840 | tf_op jit(solution)/shard_map/all_gather | solution.py:81
  126.4 149.9 %all-gather.21.cloned.1.call-start = ((), (), s32[]{:S(2)}) async-start(), calls=%async_computation.20 | async-start | bytes 5898240 | tf_op jit(solution)/shard_map/all_gather | solution.py:82
  140.1 222.7 %all-gather.23.cloned.1.call-start = ((), (), s32[]{:S(2)}) async-start(), calls=%async_computation.21 | async-start | bytes 5898240 | tf_op jit(solution)/shard_map/all_gather | solution.py:83
  150.2 295.3 %all-gather.25.cloned.1.call-start = ((), (), s32[]{:S(2)}) async-start(), calls=%async_computation.22 | async-start | bytes 5529600 | tf_op jit(solution)/shard_map/all_gather | solution.py:84
  158.5 545.3 %reduce-scatter.30.cloned.1.call-start = ((), (), s32[]{:S(2)}) async-start(), calls=%async_computation.23 | async-start | bytes 3276800 | tf_op jit(solution)/shard_map/reduce_scatter | solution.py:293
  241.4 222.0 %copy-start.1 = (f32[512,960]{0,1:T(8,128)}, f32[512,960]{0,1:T(8,128)S(1)}, u32[]{:S(2)}) copy-start(f32[512,960]{0,1:T(8,128)S(1)} %get-tuple-element.583) | copy-start | bytes 5898244
  670.8 70.4 %reduce-scatter.32.cloned.1.call-start = ((), (), s32[]{:S(2)}) async-start(), calls=%async_computation.24 | async-start | bytes 3276800 | tf_op jit(solution)/shard_map/reduce_scatter | solution.py:296
  671.6 137.3 %reduce-scatter.36.cloned.1.call-start = ((), (), s32[]{:S(2)}) async-start(), calls=%async_computation.26 | async-start | bytes 1474560 | tf_op jit(solution)/shard_map/reduce_scatter | solution.py:95
  706.8 168.9 %reduce-scatter.38.cloned.1.call-start = ((), (), s32[]{:S(2)}) async-start(), calls=%async_computation.27 | async-start | bytes 1474560 | tf_op jit(solution)/shard_map/reduce_scatter | solution.py:96
  744.1 311.9 %reduce-scatter.42.cloned.1.call-start = ((), (), s32[]{:S(2)}) async-start(), calls=%async_computation.29 | async-start | bytes 11796480 | tf_op jit(solution)/shard_map/reduce_scatter | solution.py:98
  753.0 483.8 %reduce-scatter.44.cloned.1.call-start = ((), (), s32[]{:S(2)}) async-start(), calls=%async_computation.30 | async-start | bytes 11796480 | tf_op jit(solution)/shard_map/reduce_scatter | solution.py:99
  762.0 561.7 %reduce-scatter.50.cloned.1.call-start = ((), (), s32[]{:S(2)}) async-start(), calls=%async_computation.33 | async-start | bytes 4423680
  768.2 643.6 %reduce-scatter.56.cloned.1.call-start = ((), (), s32[]{:S(2)}) async-start(), calls=%async_computation.36 | async-start | bytes 4423680
  772.6 811.4 %reduce-scatter.46.cloned.1.call-start = ((), (), s32[]{:S(2)}) async-start(), calls=%async_computation.31 | async-start | bytes 11059200 | tf_op jit(solution)/shard_map/reduce_scatter | solution.py:100
  781.3 845.2 %reduce-scatter.52.cloned.1.call-start = ((), (), s32[]{:S(2)}) async-start(), calls=%async_computation.34 | async-start | bytes 614400
  810.8 819.9 %reduce-scatter.54.cloned.1.call-start = ((), (), s32[]{:S(2)}) async-start(), calls=%async_computation.35 | async-start | bytes 614400
  877.6 783.3 %reduce-scatter.58.cloned.1.call-start = ((), (), s32[]{:S(2)}) async-start(), calls=%async_computation.37 | async-start | bytes 1843200
  1058.9 632.1 %reduce-scatter.60.cloned.1.call-start = ((), (), s32[]{:S(2)}) async-start(), calls=%async_computation.38 | async-start | bytes 1843200
  1239.8 475.8 %reduce-scatter.34.cloned.1.call-start = ((), (), s32[]{:S(2)}) async-start(), calls=%async_computation.25 | async-start | bytes 614400 | tf_op jit(solution)/shard_map/reduce_scatter | solution.py:104
  1325.9 414.3 %reduce-scatter.40.cloned.1.call-start = ((), (), s32[]{:S(2)}) async-start(), calls=%async_computation.28 | async-start | bytes 614400 | tf_op jit(solution)/shard_map/reduce_scatter | solution.py:107
  1413.9 355.5 %reduce-scatter.48.cloned.1.call-start = ((), (), s32[]{:S(2)}) async-start(), calls=%async_computation.32 | async-start | bytes 1536000 | tf_op jit(solution)/shard_map/reduce_scatter | solution.py:110
  (24 other events, 355.1 us)
Sparse Core Ops, SparseCore 0:
  15.7 58.8 all-gather.12
  80.3 15.4 all-gather.14
  119.9 18.6 all-gather.16
  141.2 47.6 all-gather.18
  191.0 85.2 all-gather.20
  278.4 84.4 all-gather.22
  365.0 80.4 all-gather.24
  671.0 32.8 reduce-scatter.29
  706.6 34.6 reduce-scatter.31
  744.5 64.3 reduce-scatter.35
  812.3 63.3 reduce-scatter.37
  879.1 176.8 reduce-scatter.41
  1059.6 177.1 reduce-scatter.43
  1240.3 83.4 reduce-scatter.49
  1327.8 84.0 reduce-scatter.55
  1415.3 168.6 reduce-scatter.45
  1586.3 20.5 reduce-scatter.51
  1609.3 21.4 reduce-scatter.53
  1633.3 27.5 reduce-scatter.57
  1663.5 27.5 reduce-scatter.59
  1694.1 21.4 reduce-scatter.33
  1718.7 21.4 reduce-scatter.39
  1743.3 26.0 reduce-scatter.47
where the time goes:
time: 1790 us; the launch traced here: 1780 us
  waiting for transfers between devices  1180 us (66%)
  matrix products  330 us (18%)
  blocking collectives  164 us (9%)
  local copies, waits for them, and re-layouts  56.2 us (3%)
  other arithmetic  31 us (2%)
    unnamed x29, waiting for transfers between devices  230 us
    reduce_scatter x1, waiting for transfers between devices, reduce_grads(): lax.psum_scatter(gate_term, 'dp', scatter_dimension=1, tiled=True)  178 us
    reduce_scatter x1, waiting for transfers between devices, reduce_grads(): lax.psum_scatter(up_term, 'dp', scatter_dimension=1, tiled=True)  178 us
    reduce_scatter x1, waiting for transfers between devices, reduce_grads(): lax.psum_scatter(down_term, 'dp', scatter_dimension=1, tiled=True)  169 us
    dot_general x35, matrix products, outer_sum(): lax.dot_general(operand, other, (((0,), (0,)), ((), ())), preferred_eleme...  95.4 us
    dot_general x30, matrix products, head_scores(): jnp.einsum('qd,kd->qk', query_one, key_one, preferred_element_type=jnp.fl...  79 us
    all_gather x1, waiting for transfers between devices, gather_weights(): lax.all_gather(row_parts[5], 'dp', axis=1, tiled=True)  78.4 us
    all_gather x1, waiting for transfers between devices, gather_weights(): lax.all_gather(row_parts[6], 'dp', axis=1, tiled=True)  74.7 us
  transfers between devices with their start and end apart: 23, of which 18 were waited for; matrix products, arithmetic and copies ran while one was open for 11% of the time, Pallas kernels for 0%

commit v1 on v0

v1 whole, which is shorter than its diff:
```python
import math

import jax
import jax.numpy as jnp
from jax import lax
from jax.experimental import pallas as pl
from jax.experimental.pallas import tpu as pltpu
from jax.sharding import PartitionSpec as P

D = 960
HEADS = 15
KV_HEADS = 5
HEAD_DIM = 64
KV_WIDTH = 320
RATIO = HEADS // KV_HEADS
HALF = HEAD_DIM // 2

norm_eps = 1e-05
masked_value = -1e30
score_scale = 0.125
score_scale_two = score_scale * math.log2(math.e)

F32 = jnp.float32
BF16 = jnp.bfloat16
FORWARD_CALLS = ((0, 5),)
BACKWARD_CALLS = ((0, 1), (1, 1), (2, 1), (3, 1), (4, 1))


def dot(a, b, contract_a, contract_b):
    return lax.dot_general(
        a, b, ((contract_a, contract_b), ((), ())), preferred_element_type=F32
    )


def strides_of(size):
    strides, stride = [], size // 2
    while stride:
        strides.append(stride)
        stride //= 2
    return strides


def swap(value, axis, size, stride):
    return lax.ppermute(value, axis, [(i, i ^ stride) for i in range(size)])


def gather_rows(values, size):
    gathered = values[None]
    for stride in strides_of(size):
        gathered = jnp.concatenate([gathered, swap(gathered, "fsdp", size, stride)], axis=0)
    return gathered


def relative_of(position, size):
    relative = 0
    for place, stride in enumerate(strides_of(size)):
        relative += ((position >> place) & 1) * stride
    return relative


def take(addend, choice):
    array, labels, fixed = addend
    fixed = {**fixed, **choice}
    starts = [fixed.get(label, 0) for label in labels] + [0, 0]
    sizes = [1 if label in fixed else 2 for label in labels] + list(array.shape[-2:])
    piece = lax.dynamic_slice(array, starts, sizes)
    return piece.reshape([n for n, label in zip(sizes, labels) if label not in fixed] + list(array.shape[-2:]))


def reduce_pieces(send, keep, order, sizes, my_bits):
    labels = [bit for bit in my_bits if bit != order[0]]
    received = swap(send, order[0][0], sizes[order[0][0]], order[0][1])
    addends = [(keep, labels, {}), (received, labels, {})]
    for bit in order[1:]:
        other = sum(take(a, {bit: 1 - my_bits[bit]}).astype(F32) for a in addends)
        received = swap(other.astype(BF16), bit[0], sizes[bit[0]], bit[1])
        addends = [(a, l, {**f, bit: my_bits[bit]}) for a, l, f in addends]
        labels = [label for label in labels if label != bit]
        addends.append((received, labels, {}))
    return sum(take(a, {}).astype(F32) for a in addends)


def place_of(relative, size):
    place = 0
    for at, stride in enumerate(strides_of(size)):
        bit = lax.rem(lax.div(relative, stride), 2)
        place = place + bit * (1 << at)
    return place


def visible(start, first_query, first_key, keys, queries):
    key_row = first_key + lax.broadcasted_iota(jnp.int32, (keys, queries), 0)
    query_row = first_query + lax.broadcasted_iota(jnp.int32, (keys, queries), 1)
    return (key_row >= start) & (key_row <= query_row)


def forward_kernel(me_ref, start_ref, q_ref, k_ref, v_ref, o_ref, lse_ref, keys, total, top, acc):
    parts, _, chunk = k_ref.shape
    rows = q_ref.shape[1]
    me = me_ref[0]
    for part in range(parts):
        keys[part] = k_ref[part].T
    start = start_ref[...]

    def block(part_at, first, later):
        at = place_of(jnp.bitwise_xor(part_at, me), parts)
        if first:
            shown = visible(start, me * rows, part_at * chunk, chunk, rows)
        else:
            shown = (part_at * chunk + lax.broadcasted_iota(jnp.int32, (chunk, rows), 0)) >= start
        for h in range(RATIO):
            head = slice(h * HEAD_DIM, (h + 1) * HEAD_DIM)
            scores = dot(keys[at], q_ref[head, :], (1,), (0,)) * score_scale_two
            scores = jnp.where(shown, scores, masked_value)
            high = jnp.max(scores, axis=0, keepdims=True)
            if not first:
                before = top[h : h + 1, :]
                high = jnp.maximum(high, before)
                shrink = jnp.exp2(before - high)
            probs = jnp.exp2(scores - high)
            sums = jnp.sum(probs, axis=0, keepdims=True)
            mixed = dot(v_ref[at], probs.astype(BF16), (1,), (0,))
            if first:
                total[h : h + 1, :] = sums
                acc[head, :] = mixed
            else:
                total[h : h + 1, :] = total[h : h + 1, :] * shrink + sums
                acc[head, :] = acc[head, :] * shrink + mixed
            top[h : h + 1, :] = high

    block(me, True, False)

    def later(part_at, carry):
        block(part_at, False, True)
        return carry

    lax.fori_loop(0, me, later, 0)
    for h in range(RATIO):
        head = slice(h * HEAD_DIM, (h + 1) * HEAD_DIM)
        sums = total[h : h + 1, :]
        o_ref[head, :] = (acc[head, :] / sums).astype(BF16)
        lse_ref[0, h : h + 1, :] = top[h : h + 1, :] + jnp.log2(sums)


def backward_kernel(
    me_ref, start_ref, cos_ref, sin_ref, q_ref, k_ref, v_ref, o_ref, do_ref, lse_ref,
    dq_ref, dk_ref, dv_ref, keys, values, acc, delta
):
    parts, _, chunk = k_ref.shape
    rows = q_ref.shape[1]
    me = me_ref[0]
    for part in range(parts):
        keys[part] = k_ref[part].T
        values[part] = v_ref[part].T
    start = start_ref[...]
    for h in range(RATIO):
        head = slice(h * HEAD_DIM, (h + 1) * HEAD_DIM)
        delta[h : h + 1, :] = jnp.sum(
            o_ref[head, :].astype(F32) * do_ref[head, :].astype(F32), axis=0, keepdims=True
        )

    def block(part_at, first):
        at = place_of(jnp.bitwise_xor(part_at, me), parts)
        if first:
            shown = visible(start, me * rows, part_at * chunk, chunk, rows)
        else:
            shown = (part_at * chunk + lax.broadcasted_iota(jnp.int32, (chunk, rows), 0)) >= start
        dk = dv = None
        for h in range(RATIO):
            head = slice(h * HEAD_DIM, (h + 1) * HEAD_DIM)
            query, grad = q_ref[head, :], do_ref[head, :]
            scores = dot(keys[at], query, (1,), (0,)) * score_scale_two
            scores = jnp.where(shown, scores, masked_value)
            probs = jnp.exp2(scores - lse_ref[0, h : h + 1, :])
            grad_probs = dot(values[at], grad, (1,), (0,))
            grad_scores = (probs * (grad_probs - delta[h : h + 1, :])).astype(BF16)
            dq = dot(k_ref[at], grad_scores, (1,), (0,))
            if first:
                acc[head, :] = dq
            else:
                acc[head, :] = acc[head, :] + dq
            dk_one = dot(query, grad_scores, (1,), (1,))
            dv_one = dot(grad, probs.astype(BF16), (1,), (1,))
            dk = dk_one if dk is None else dk + dk_one
            dv = dv_one if dv is None else dv + dv_one
        dk_ref[at] = (dk * score_scale).astype(BF16)
        dv_ref[at] = dv.astype(BF16)

    block(me, True)

    def later(part_at, carry):
        block(part_at, False)
        return carry

    lax.fori_loop(0, me, later, 0)

    def unseen(part_at, carry):
        at = place_of(jnp.bitwise_xor(part_at, me), parts)
        dk_ref[at] = jnp.zeros((HEAD_DIM, chunk), BF16)
        dv_ref[at] = jnp.zeros((HEAD_DIM, chunk), BF16)
        return carry

    lax.fori_loop(me + 1, parts, unseen, 0)
    cosine, sine = cos_ref[...], sin_ref[...]
    for h in range(RATIO):
        low = acc[h * HEAD_DIM : h * HEAD_DIM + HALF, :] * score_scale
        high = acc[h * HEAD_DIM + HALF : (h + 1) * HEAD_DIM, :] * score_scale
        dq_ref[h * HEAD_DIM : h * HEAD_DIM + HALF, :] = (low * cosine + high * sine).astype(BF16)
        dq_ref[h * HEAD_DIM + HALF : (h + 1) * HEAD_DIM, :] = (high * cosine - low * sine).astype(BF16)


def kernel_call(kernel, heads, ins, outs, scratch, cost):
    return pl.pallas_call(
        kernel,
        grid_spec=pltpu.PrefetchScalarGridSpec(
            num_scalar_prefetch=1, grid=(heads,), in_specs=ins,
            out_specs=[spec for spec, _ in outs], scratch_shapes=scratch,
        ),
        out_shape=[shape for _, shape in outs],
        cost_estimate=cost,
        compiler_params=pltpu.CompilerParams(vmem_limit_bytes=48 * 1024 * 1024),
    )


def attend_forward(me, start, query, keys_values):
    parts, _, chunk = keys_values.shape
    rows = query.shape[1]
    group = RATIO * HEAD_DIM
    attended, totals = [], []
    for first, count in FORWARD_CALLS:
        work = 2 * count * RATIO * rows * parts * chunk
        out, lse = kernel_call(
            forward_kernel,
            count,
            [
                pl.BlockSpec((1, rows), lambda g, s: (0, 0)),
                pl.BlockSpec((group, rows), lambda g, s, first=first: (g + first, 0)),
                pl.BlockSpec((parts, HEAD_DIM, chunk), lambda g, s, first=first: (0, g + first, 0)),
                pl.BlockSpec((parts, HEAD_DIM, chunk), lambda g, s, first=first: (0, KV_HEADS + g + first, 0)),
            ],
            [
                (pl.BlockSpec((group, rows), lambda g, s: (g, 0)), jax.ShapeDtypeStruct((count * group, rows), BF16)),
                (pl.BlockSpec((1, RATIO, rows), lambda g, s: (g, 0, 0)), jax.ShapeDtypeStruct((count, RATIO, rows), F32)),
            ],
            [
                pltpu.VMEM((parts, chunk, HEAD_DIM), BF16),
                pltpu.VMEM((8, rows), F32),
                pltpu.VMEM((8, rows), F32),
                pltpu.VMEM((group, rows), F32),
            ],
            pl.CostEstimate(flops=8 * HEAD_DIM * work, bytes_accessed=4_000_000, transcendentals=work // 2),
        )(me, start, query, keys_values, keys_values)
        attended.append(out)
        totals.append(lse)
    return jnp.concatenate(attended, axis=0), jnp.concatenate(totals, axis=0)


def attend_backward(me, start, cosine, sine, query, keys_values, attended, grad_attended, totals):
    parts, _, chunk = keys_values.shape
    rows = query.shape[1]
    group = RATIO * HEAD_DIM
    pieces = []
    for first, count in BACKWARD_CALLS:
        work = 2 * count * RATIO * rows * parts * chunk
        whole = lambda g, s: (0, 0)
        by_group = lambda g, s, first=first: (g + first, 0)
        pieces.append(
            kernel_call(
                backward_kernel,
                count,
                [
                    pl.BlockSpec((1, rows), whole),
                    pl.BlockSpec((HALF, rows), whole),
                    pl.BlockSpec((HALF, rows), whole),
                    pl.BlockSpec((group, rows), by_group),
                    pl.BlockSpec((parts, HEAD_DIM, chunk), lambda g, s, first=first: (0, g + first, 0)),
                    pl.BlockSpec((parts, HEAD_DIM, chunk), lambda g, s, first=first: (0, KV_HEADS + g + first, 0)),
                    pl.BlockSpec((group, rows), by_group),
                    pl.BlockSpec((group, rows), by_group),
                    pl.BlockSpec((1, RATIO, rows), lambda g, s, first=first: (g + first, 0, 0)),
                ],
                [
                    (pl.BlockSpec((group, rows), lambda g, s: (g, 0)), jax.ShapeDtypeStruct((count * group, rows), BF16)),
                    (pl.BlockSpec((parts, HEAD_DIM, chunk), lambda g, s: (0, g, 0)), jax.ShapeDtypeStruct((parts, count * HEAD_DIM, chunk), BF16)),
                    (pl.BlockSpec((parts, HEAD_DIM, chunk), lambda g, s: (0, g, 0)), jax.ShapeDtypeStruct((parts, count * HEAD_DIM, chunk), BF16)),
                ],
                [
                    pltpu.VMEM((parts, chunk, HEAD_DIM), BF16),
                    pltpu.VMEM((parts, chunk, HEAD_DIM), BF16),
                    pltpu.VMEM((group, rows), F32),
                    pltpu.VMEM((8, rows), F32),
                ],
                pl.CostEstimate(flops=20 * HEAD_DIM * work, bytes_accessed=4_000_000, transcendentals=work // 2),
            )(me, start, cosine, sine, query, keys_values, keys_values, attended, grad_attended, totals)
        )
    grad_query = jnp.concatenate([p[0] for p in pieces], axis=0)
    grad_keys_values = jnp.concatenate([p[1] for p in pieces] + [p[2] for p in pieces], axis=1)
    return grad_query, grad_keys_values


def rotate(values, cosine, sine):
    heads = values.reshape(-1, 2, HALF, values.shape[-1])
    low, high = heads[:, 0], heads[:, 1]
    return jnp.stack([low * cosine - high * sine, high * cosine + low * sine], axis=1).reshape(values.shape)


def rotate_back(values, cosine, sine):
    return rotate(values, cosine, -sine)


def make_layer(dp, fsdp):
    sizes = {"dp": dp, "fsdp": fsdp}
    dp_bits = [("dp", stride) for stride in strides_of(dp)]
    fsdp_bits = [("fsdp", stride) for stride in strides_of(fsdp)]
    near = fsdp_bits[-1]
    far = fsdp_bits[:-1]
    order_one = [near] + far[::-1] + dp_bits[::-1]
    order_two = [near] + dp_bits[::-1][:1] + far[::-1] + dp_bits[::-1][1:]

    def layer(
        tokens, norm_gains, query_weight, key_weight, value_weight, out_weight,
        gate_weight, up_weight, down_weight, segment_ids, out_grad
    ):
        rows = tokens.shape[0]
        cols = norm_gains.shape[1]
        depth = query_weight.shape[0]
        kv_cols = key_weight.shape[1]
        ff = gate_weight.shape[1] * dp
        ff_part = down_weight.shape[0]
        me = lax.axis_index("fsdp").astype(jnp.int32)
        me_dp = lax.axis_index("dp").astype(jnp.int32)
        my_bits = {bit: 0 for bit in fsdp_bits}
        my_bits.update({bit: lax.rem(lax.div(me_dp, bit[1]), 2) for bit in dp_bits})

        def gather(piece):
            return lax.all_gather(piece, ("fsdp", "dp"), axis=0, tiled=False).reshape(
                (fsdp, dp) + piece.shape
            )

        gain_row = jnp.concatenate([norm_gains[0], norm_gains[1]])
        gain_rows = jnp.pad(gain_row[None, :], ((0, 7), (0, depth - 2 * cols)))
        first = gather(jnp.concatenate([query_weight.T, key_weight.T, value_weight.T, gain_rows], axis=0))
        kv_end = cols + 2 * kv_cols
        w_query = first[:, :, :cols].reshape(fsdp, D, depth)
        w_key = first[:, :, cols : cols + kv_cols].reshape(fsdp, KV_WIDTH, depth)
        w_value = first[:, :, cols + kv_cols : kv_end].reshape(fsdp, KV_WIDTH, depth)
        gain_one = first[0, :, kv_end, :cols].reshape(1, D).astype(F32)
        gain_two = first[0, :, kv_end, cols : 2 * cols].reshape(1, D).astype(F32)
        w_out = gather(out_weight.T).reshape(fsdp, D, depth)
        w_gate = gather(gate_weight.T).reshape(fsdp, ff, depth)
        w_up = gather(up_weight.T).reshape(fsdp, ff, depth)
        w_down = gather(down_weight.T).reshape(fsdp, D, ff_part)

        ends = [jnp.sum((segment_ids < which).astype(jnp.int32)) for which in (1, 2)]
        local_ids = lax.dynamic_slice_in_dim(segment_ids, me * rows, rows)
        start = jnp.where(local_ids == 0, 0, jnp.where(local_ids == 1, ends[0], ends[1]))
        positions = me * rows + jnp.arange(rows, dtype=jnp.int32) - start
        frequency = jnp.exp(jnp.arange(HALF, dtype=F32) * (-2.0 * math.log(10000.0) / HEAD_DIM))
        angles = frequency[:, None] * positions.astype(F32)[None, :]
        cosine, sine = jnp.cos(angles), jnp.sin(angles)
        start = start[None, :]
        me_row = me[None]

        def chunks(values):
            return values.reshape(rows, fsdp, -1).transpose(1, 0, 2)

        def own_order(values):
            return [
                lax.dynamic_index_in_dim(values, jnp.bitwise_xor(me, j), 0, keepdims=False)
                for j in range(fsdp)
            ]

        inputs = tokens.astype(F32)
        inv_one = lax.rsqrt(jnp.mean(inputs * inputs, axis=1, keepdims=True) + norm_eps)
        normed = (inputs * inv_one * gain_one).astype(BF16)
        normed_parts = chunks(normed)

        def project(weight, parts):
            return dot(weight, parts, (0, 2), (0, 2))

        query = rotate(project(w_query, normed_parts), cosine, sine).astype(BF16)
        key = rotate(project(w_key, normed_parts), cosine, sine).astype(BF16)
        value = project(w_value, normed_parts).astype(BF16)
        keys_values = gather_rows(jnp.concatenate([key, value], axis=0), fsdp)
        attended, totals = attend_forward(me_row, start, query, keys_values)
        attended_parts = attended.reshape(fsdp, depth, rows)
        hidden = inputs + dot(attended_parts, w_out, (0, 1), (0, 2))
        inv_two = lax.rsqrt(jnp.mean(hidden * hidden, axis=1, keepdims=True) + norm_eps)
        normed_two = (hidden * inv_two * gain_two).astype(BF16)
        two_parts = chunks(normed_two)
        gate_act = dot(two_parts, w_gate, (0, 2), (0, 2))
        up_act = dot(two_parts, w_up, (0, 2), (0, 2))
        sigmoid = jax.nn.sigmoid(gate_act)
        mixed = (gate_act * sigmoid * up_act).astype(BF16)
        mixed_parts = chunks(mixed)
        output = hidden + dot(mixed_parts, w_down, (0, 2), (0, 2))

        def reduce(left, right_parts, order, contract=(0,), contract_right=(0,)):
            halves = []
            for wanted in (1, 0):
                terms = [
                    dot(left, part, contract, contract_right).astype(BF16)
                    for j, part in enumerate(right_parts)
                    if j % 2 == wanted
                ]
                whole = jnp.stack(terms)
                halves.append(
                    whole.reshape([2] * (len(far) + len(dp_bits)) + [-1, whole.shape[-1]])
                )
            return reduce_pieces(halves[0], halves[1], order, sizes, my_bits)

        grad_output = out_grad.astype(F32)
        sum_down = reduce(out_grad, own_order(mixed_parts), order_one)
        grad_mixed = dot(out_grad, w_down, (1,), (1,)).reshape(rows, ff)
        grad_gate = (grad_mixed * up_act * sigmoid * (1.0 + gate_act * (1.0 - sigmoid))).astype(BF16)
        grad_up = (grad_mixed * gate_act * sigmoid).astype(BF16)
        two_own = own_order(two_parts)
        sum_gate = reduce(grad_gate, two_own, order_two)
        sum_up = reduce(grad_up, two_own, order_one)
        grad_two = (dot(grad_gate, w_gate, (1,), (1,)) + dot(grad_up, w_up, (1,), (1,))).reshape(rows, D)
        weighted_two = grad_two * gain_two
        grad_gain_two = jnp.sum(grad_two * hidden * inv_two, axis=0)
        grad_hidden = (
            grad_output
            + inv_two * weighted_two
            - hidden * (inv_two * inv_two * inv_two) * jnp.mean(weighted_two * hidden, axis=1, keepdims=True)
        )
        branch_grad = grad_hidden.astype(BF16)
        sum_out = reduce(branch_grad, own_order(attended_parts), order_two, (0,), (1,))
        grad_attended = dot(w_out, branch_grad, (1,), (1,)).astype(BF16).reshape(D, rows)
        grad_query, grad_keys_values = attend_backward(
            me_row, start, cosine, sine, query, keys_values, attended, grad_attended, totals
        )
        normed_own = own_order(normed_parts)
        sum_query = reduce(grad_query, normed_own, order_two, (1,), (0,))

        mine = [grad_keys_values]
        for stride in strides_of(fsdp)[::-1]:
            half = mine[0].shape[0] // 2
            other = sum(m[half:].astype(F32) for m in mine).astype(BF16)
            mine = [m[:half] for m in mine] + [swap(other, "fsdp", fsdp, stride)]
        key_value_sum = sum(m[0].astype(F32) for m in mine)
        grad_key = rotate_back(key_value_sum[:KV_WIDTH], cosine, sine).astype(BF16)
        grad_value = key_value_sum[KV_WIDTH:].astype(BF16)
        grad_normed = (
            dot(grad_query, w_query, (0,), (1,))
            + dot(grad_key, w_key, (0,), (1,))
            + dot(grad_value, w_value, (0,), (1,))
        ).reshape(rows, D)
        weighted_one = grad_normed * gain_one
        grad_gain_one = jnp.sum(grad_normed * inputs * inv_one, axis=0)
        input_grad = (
            grad_hidden
            + inv_one * weighted_one
            - inputs * (inv_one * inv_one * inv_one) * jnp.mean(weighted_one * inputs, axis=1, keepdims=True)
        )
        both = jnp.concatenate(
            [grad_key.reshape(dp, kv_cols, rows), grad_value.reshape(dp, kv_cols, rows)], axis=1
        )
        gains_piece = jnp.concatenate(
            [grad_gain_one.reshape(dp, 1, cols), grad_gain_two.reshape(dp, 1, cols)], axis=2
        )
        gains_piece = jnp.pad(gains_piece, ((0, 0), (0, 7), (0, depth - 2 * cols))).astype(BF16)
        halves = []
        for wanted in (1, 0):
            terms = [
                jnp.concatenate(
                    [dot(both, part, (2,), (0,)).astype(BF16), gains_piece], axis=1
                )
                for j, part in enumerate(normed_own)
                if j % 2 == wanted
            ]
            whole = jnp.stack(terms)
            halves.append(whole.reshape([2] * (len(far) + len(dp_bits)) + list(whole.shape[-2:])))
        last = reduce_pieces(halves[0], halves[1], order_one, sizes, my_bits)
        return (
            output.astype(BF16),
            input_grad,
            last[2 * kv_cols, : 2 * cols].reshape(2, cols),
            sum_query.T,
            last[:kv_cols].T,
            last[kv_cols : 2 * kv_cols].T,
            sum_out.T,
            sum_gate.T,
            sum_up.T,
            sum_down.T,
        )

    return layer


def solution(mesh):
    weight = P("fsdp", "dp")
    token = P(("dp", "fsdp"), None)
    gains = P(None, "dp")
    return jax.shard_map(
        make_layer(mesh.shape["dp"], mesh.shape["fsdp"]),
        mesh=mesh,
        in_specs=(token, gains) + (weight,) * 7 + (P("dp"), token),
        out_specs=(token, token, gains) + (weight,) * 7,
        check_vma=False,
    )
```

time: 1790 us -> 693 us (0.39)
  waiting for transfers between devices: 1180 us -> 334 us
  matrix products: 330 us -> 82.3 us
  blocking collectives: 164 us -> 0 us
  starting transfers between devices: 1.42 us -> 63.5 us
  other arithmetic: 31 us -> 77.6 us
  local copies, waits for them, and re-layouts: 56.2 us -> 87.1 us
  Pallas kernels: 0 us -> 28.9 us
    reduce_scatter x10 -> x0, waiting for transfers between devices: 760 us -> none  [the longest x1 178 us: reduce_grads(): lax.psum_scatter(gate_term, 'dp', scatter_dimension=1, tiled=True)]
    dot_general x124 -> x34, matrix products: 322 us -> 71.4 us  [dot(): lax.dot_general(a, b, ((contract_a, contract_b), ((), ())), preferred_ele...]
    unnamed x29 -> x5, waiting for transfers between devices: 230 us -> 1.77 us
    all_gather x10 -> x0, blocking collectives: 138 us -> none  [the longest x1 33 us: gather_weights(): lax.all_gather(row_parts[1], 'dp', axis=1, tiled=True)]
    ppermute x0 -> x34, waiting for transfers between devices: none -> 95.8 us  [swap(): return lax.ppermute(value, axis, [(i, i ^ stride) for i in range(size)])]
    ppermute x0 -> x34, starting transfers between devices: none -> 63.3 us  [swap(): return lax.ppermute(value, axis, [(i, i ^ stride) for i in range(size)])]
    all_gather x7 -> x5, waiting for transfers between devices: 187 us -> 236 us  [gather(): lax.all_gather(piece, ('fsdp', 'dp'), axis=0, tiled=False)]
    another operation x2 -> x16, local copies, waits for them, and re-layouts: 3.66 us -> 35.9 us  [the longest x11 15.8 us: reduce(): whole = jnp.stack(terms)]
  transfers between devices with their start and end apart: 23 -> 39, of which waited for: 18 -> 17; matrix products, arithmetic and copies ran while one was open for 11% -> 23% of each run, Pallas kernels for 0% -> 1%
where the time goes in v1:
time: 693 us; the launch traced here: 688 us
  waiting for transfers between devices  334 us (48%)
  local copies, waits for them, and re-layouts  87.1 us (13%)
  matrix products  82.3 us (12%)
  other arithmetic  77.6 us (11%)
  starting transfers between devices  63.5 us (9%)
  Pallas kernels  28.9 us (4%)
  between operations  15.3 us (2%)
    all_gather x5, waiting for transfers between devices, gather(): lax.all_gather(piece, ('fsdp', 'dp'), axis=0, tiled=False)  236 us
    ppermute x34, waiting for transfers between devices, swap(): return lax.ppermute(value, axis, [(i, i ^ stride) for i in range(size)])  95.8 us
    dot_general x34, matrix products, dot(): lax.dot_general(a, b, ((contract_a, contract_b), ((), ())), preferred_ele...  71.4 us
    ppermute x34, starting transfers between devices, swap(): return lax.ppermute(value, axis, [(i, i ^ stride) for i in range(size)])  63.3 us
    convert_element_type x24, other arithmetic, reduce_pieces(): received = swap(other.astype(BF16), bit[0], sizes[bit[0]], bit[1])  29.9 us
    pallas_call x5, Pallas kernels, attend_backward(): kernel_call(backward_kernel, count, [pl.BlockSpec((1, rows), whole), pl.B...  19.8 us
    convert_element_type x8, local copies, waits for them, and re-layouts, reduce(): dot(left, part, contract, contract_right).astype(BF16)  17.1 us
    another operation x11, local copies, waits for them, and re-layouts, reduce(): whole = jnp.stack(terms)  15.8 us
  transfers between devices with their start and end apart: 39, of which 17 were waited for; matrix products, arithmetic and copies ran while one was open for 23% of the time, Pallas kernels for 1%

profile of v1, /device:TPU:0, one launch (start us, length us, event | category | flops | bytes accessed | tf_op | source)
XLA Modules:
  0.0 688.1 jit_solution(6949670165566609650)
XLA Ops:
  20.5 53.6 %all-gather.11.cloned.1.call-done = bf16[6656,240]{1,0:T(8,128)(2,1)} async-done(((bf16[208,240]{1,0:T(8,128)(2,1)}), bf16[6656,240]{1,0:T(8,128)(2,1)}) %all-gather.11.cloned.1.call-update) | async-done | bytes 3194896 | tf_op jit(solution)/shard_map/all_gather | solution.py:336
  79.9 15.9 %collective-permute-done = bf16[1,640,512]{2,1,0:T(8,128)(2,1)S(1)} collective-permute-done((bf16[1,640,512]{2,1,0:T(8,128)(2,1)S(1)}, bf16[1,640,512]{2,1,0:T(8,128)(2,1)S(1)}, u32[]{:S(2)}, u32[]{:S(2)}) %collective-permute-start) | collective-permute-done | bytes 655392 | tf_op jit(solution)/shard_map/ppermute | solution.py:44
  97.0 35.9 %all-gather.13.cloned.1.call-done = bf16[3840,240]{1,0:T(8,128)(2,1)} async-done(((bf16[120,240]{1,0:T(8,128)(2,1)}), bf16[3840,240]{1,0:T(8,128)(2,1)}) %all-gather.13.cloned.1.call-update) | async-done | bytes 1843216 | tf_op jit(solution)/shard_map/all_gather | solution.py:336
  146.3 9.1 %shard_map.186 = (bf16[960,512]{1,0:T(8,128)(2,1)S(1)}, f32[5,3,512]{2,1,0:T(4,128)S(1)}) custom-call(s32[1]{0:T(128)} %bitcast.10.me_ref, s32[1,512]{1,0:T(1,128)S(1)} %bitcast.624, bf16[960,512]{1,0:T(8,128)(2,1)S(1)} %bitcast.613, bf16[4,640,512]{2,1,0:T(8,128)(2,1)S(1)} %pad_maximum_fusion.k_ref.v_ref, bf16[4,640,512]{2,1,0:T(8,128)(2,1)S(1)} %pad_maximum_fusion.k_ref.v_ref), custom_call_target="tpu_custom_call" | custom-call | flops 16106127360 | bytes 4000000 | tf_op jit(solution)/shard_map/pallas_call | solution.py:232
  159.2 41.1 %all-gather.17.cloned.1.call-done = bf16[10240,240]{1,0:T(8,128)(2,1)} async-done(((bf16[320,240]{1,0:T(8,128)(2,1)}), bf16[10240,240]{1,0:T(8,128)(2,1)}) %all-gather.17.cloned.1.call-update) | async-done | bytes 4915216 | tf_op jit(solution)/shard_map/all_gather | solution.py:336
  200.3 7.7 %copy.255 = bf16[4,2560,240]{1,2,0:T(8,128)(2,1)} copy(bf16[4,2560,240]{2,1,0:T(8,128)(2,1)} %bitcast.685) | data formatting | bytes 9830400 | tf_op jit(solution)/shard_map/reshape;reshape | solution.py:351
  208.0 59.3 %all-gather.15.cloned.1.call-done = bf16[10240,240]{1,0:T(8,128)(2,1)} async-done(((bf16[320,240]{1,0:T(8,128)(2,1)}), bf16[10240,240]{1,0:T(8,128)(2,1)}) %all-gather.15.cloned.1.call-update) | async-done | bytes 4915216 | tf_op jit(solution)/shard_map/all_gather | solution.py:336
  267.3 7.8 %copy.253 = bf16[4,2560,240]{1,2,0:T(8,128)(2,1)} copy(bf16[4,2560,240]{2,1,0:T(8,128)(2,1)} %bitcast.687) | data formatting | bytes 9830400 | tf_op jit(solution)/shard_map/reshape;reshape | solution.py:350
  275.1 7.4 %fusion.177 = f32[512,2560,1]{1,0,2:T(8,128)} fusion(bf16[4,512,240]{1,2,0:T(8,128)(2,1)S(1)} %bitcast.668, bf16[4,2560,240]{2,1,0:T(8,128)(2,1)} %bitcast.686), kind=kOutput, calls=%fused_computation.417 | convolution fusion | flops 2516582400 | bytes 11141120 | tf_op jit(solution)/shard_map/dot_general | solution.py:30
  282.5 4.8 fusion.176
  287.3 46.0 %all-gather.19.cloned.1.call-done = bf16[3840,640]{1,0:T(8,128)(2,1)} async-done(((bf16[120,640]{1,0:T(8,128)(2,1)}), bf16[3840,640]{1,0:T(8,128)(2,1)}) %all-gather.19.cloned.1.call-update) | async-done | bytes 4915216 | tf_op jit(solution)/shard_map/all_gather | solution.py:336
  333.2 5.5 copy.373
  338.8 11.2 %fusion.9 = (bf16[512,2560]{1,0:T(8,128)(2,1)S(1)}, bf16[512,2560]{1,0:T(8,128)(2,1)S(1)}, bf16[512,2560]{1,0:T(8,128)(2,1)}) fusion(f32[512,2560,1]{1,0,2:T(8,128)} %fusion.176, f32[512,2560,1]{1,0,2:T(8,128)} %fusion.177, bf16[512,960]{0,1:T(8,128)(2,1)S(1)} %copy-done.42, bf16[2560,960]{0,1:T(8,128)(2,1)} %bitcast.697), kind=kOutput, calls=%fused_computation.15 | convolution fusion | flops 2537553920 | bytes 24248320 | tf_op jit(solution)/shard_map/dot_general | solution.py:30
  428.2 12.6 %collective-permute-start.9 = (bf16[2,2,2,2,120,240]{4,5,1,3,2,0:T(8,128)(2,1)}, bf16[2,2,2,2,120,240]{4,5,1,3,2,0:T(8,128)(2,1)}, u32[]{:S(2)}, u32[]{:S(2)}) collective-permute-start(bf16[2,2,2,2,120,240]{4,5,1,3,2,0:T(8,128)(2,1)} %pad_maximum_fusion.6), channel_id=1, source_target_pairs={{0,1},{1,0},{2,3},{3,2},{4,5},{5,4},{6,7},{7,6},{8,9},{9,8},{10,11... | collective-permute-start | bytes 2764808 | tf_op jit(solution)/shard_map/ppermute | solution.py:44
  463.4 6.1 fusion.22
  477.9 26.1 %collective-permute-start.3 = (bf16[1,640,512]{2,1,0:T(8,128)(2,1)}, bf16[1,640,512]{2,1,0:T(8,128)(2,1)}, u32[]{:S(2)}, u32[]{:S(2)}) collective-permute-start(bf16[1,640,512]{2,1,0:T(8,128)(2,1)} %add_convert_fusion.1), channel_id=1, source_target_pairs={{0,2},{1,3},{2,0},{3,1},{4,6},{5,7},{6,4},{7,5},{8,10},{9,11},{10,... | collective-permute-start | bytes 1966088 | tf_op jit(solution)/shard_map/ppermute | solution.py:44
  527.2 6.4 collective-permute-done.11
  544.3 5.5 bitcast_multiply_fusion.6
  570.7 28.4 %collective-permute-done.5 = bf16[2,2,2,88,240]{4,3,2,1,0:T(8,128)(2,1)S(1)} collective-permute-done((bf16[2,2,2,88,240]{4,3,2,1,0:T(8,128)(2,1)S(1)}, bf16[2,2,2,88,240]{4,3,2,1,0:T(8,128)(2,1)S(1)}, u32[]{:S(2)}, u32[]{:S(2)}) %collective-permute-start.5) | collective-permute-done | bytes 337952 | tf_op jit(solution)/shard_map/ppermute | solution.py:44
  618.7 8.6 %collective-permute-done.25 = bf16[2,2,2,320,240]{4,3,2,1,0:T(8,128)(2,1)S(1)} collective-permute-done((bf16[2,2,2,320,240]{4,3,2,1,0:T(8,128)(2,1)S(1)}, bf16[2,2,2,320,240]{4,3,2,1,0:T(8,128)(2,1)S(1)}, u32[]{:S(2)}, u32[]{:S(2)}) %collective-permute-start.25) | collective-permute-done | bytes 1228832 | tf_op jit(solution)/shard_map/ppermute | solution.py:44
  630.4 9.1 %collective-permute-done.21 = bf16[2,2,320,240]{3,2,0,1:T(8,128)(2,1)S(1)} collective-permute-done((bf16[2,2,320,240]{3,2,0,1:T(8,128)(2,1)S(1)}, bf16[2,2,320,240]{3,2,0,1:T(8,128)(2,1)S(1)}, u32[]{:S(2)}, u32[]{:S(2)}) %collective-permute-start.21) | collective-permute-done | bytes 614432 | tf_op jit(solution)/shard_map/ppermute | solution.py:44
  648.9 5.5 collective-permute-done.22
  655.7 7.1 %collective-permute-done.32 = bf16[2,120,640]{2,1,0:T(8,128)(2,1)} collective-permute-done((bf16[2,120,640]{2,1,0:T(8,128)(2,1)}, bf16[2,120,640]{2,1,0:T(8,128)(2,1)}, u32[]{:S(2)}, u32[]{:S(2)}) %collective-permute-start.32) | collective-permute-done | bytes 307232 | tf_op jit(solution)/shard_map/ppermute | solution.py:44
  672.2 5.3 collective-permute-done.33
  (407 shorter events, 246.9 us)
Async XLA Ops:
  7.2 66.9 %all-gather.11.cloned.1.call-start = ((), (), s32[]{:S(2)}) async-start(), calls=%async_computation | async-start | bytes 3514368 | tf_op jit(solution)/shard_map/all_gather | solution.py:336
  10.4 122.5 %all-gather.13.cloned.1.call-start = ((), (), s32[]{:S(2)}) async-start(), calls=%async_computation.1 | async-start | bytes 2027520 | tf_op jit(solution)/shard_map/all_gather | solution.py:336
  12.0 188.3 %all-gather.17.cloned.1.call-start = ((), (), s32[]{:S(2)}) async-start(), calls=%async_computation.3 | async-start | bytes 5406720 | tf_op jit(solution)/shard_map/all_gather | solution.py:336
  12.8 254.5 %all-gather.15.cloned.1.call-start = ((), (), s32[]{:S(2)}) async-start(), calls=%async_computation.2 | async-start | bytes 5406720 | tf_op jit(solution)/shard_map/all_gather | solution.py:336
  13.4 319.9 %all-gather.19.cloned.1.call-start = ((), (), s32[]{:S(2)}) async-start(), calls=%async_computation.4 | async-start | bytes 5068800 | tf_op jit(solution)/shard_map/all_gather | solution.py:336
  97.0 47.3 %collective-permute-start.1 = (bf16[2,640,512]{2,1,0:T(8,128)(2,1)}, bf16[2,640,512]{2,1,0:T(8,128)(2,1)}, u32[]{:S(2)}, u32[]{:S(2)}) collective-permute-start(bf16[2,640,512]{2,1,0:T(8,128)(2,1)} %pad_maximum_fusion.4), channel_id=1, source_target_pairs={{0,1},{1,0},{2,3},{3,2},{4,5},{5,4},{6,7},{7,6},{8,9},{9,8},{10,11... | collective-permute-start | bytes 3932168 | tf_op jit(solution)/shard_map/ppermute | solution.py:44
  428.2 41.2 %collective-permute-start.9 = (bf16[2,2,2,2,120,240]{4,5,1,3,2,0:T(8,128)(2,1)}, bf16[2,2,2,2,120,240]{4,5,1,3,2,0:T(8,128)(2,1)}, u32[]{:S(2)}, u32[]{:S(2)}) collective-permute-start(bf16[2,2,2,2,120,240]{4,5,1,3,2,0:T(8,128)(2,1)} %pad_maximum_fusion.6), channel_id=1, source_target_pairs={{0,1},{1,0},{2,3},{3,2},{4,5},{5,4},{6,7},{7,6},{8,9},{9,8},{10,11... | collective-permute-start | bytes 2764808 | tf_op jit(solution)/shard_map/ppermute | solution.py:44
  442.4 30.5 %collective-permute-start.14 = (bf16[2,2,2,2,120,240]{4,5,1,3,2,0:T(8,128)(2,1)}, bf16[2,2,2,2,120,240]{4,5,1,3,2,0:T(8,128)(2,1)}, u32[]{:S(2)}, u32[]{:S(2)}) collective-permute-start(bf16[2,2,2,2,120,240]{4,5,1,3,2,0:T(8,128)(2,1)} %pad_maximum_fusion.7), channel_id=1, source_target_pairs={{0,1},{1,0},{2,3},{3,2},{4,5},{5,4},{6,7},{7,6},{8,9},{9,8},{10,11... | collective-permute-start | bytes 2764808 | tf_op jit(solution)/shard_map/ppermute | solution.py:44
  450.2 25.3 %collective-permute-start.2 = (bf16[2,640,512]{2,1,0:T(8,128)(2,1)}, bf16[2,640,512]{2,1,0:T(8,128)(2,1)}, u32[]{:S(2)}, u32[]{:S(2)}) collective-permute-start(bf16[2,640,512]{2,1,0:T(8,128)(2,1)} %slice.111), channel_id=1, source_target_pairs={{0,1},{1,0},{2,3},{3,2},{4,5},{5,4},{6,7},{7,6},{8,9},{9,8},{10,11... | collective-permute-start | bytes 3932168 | tf_op jit(solution)/shard_map/ppermute | solution.py:44
  471.5 52.5 %collective-permute-start.10 = (bf16[2,2,2,120,240]{3,4,2,1,0:T(8,128)(2,1)}, bf16[2,2,2,120,240]{3,4,2,1,0:T(8,128)(2,1)}, u32[]{:S(2)}, u32[]{:S(2)}) collective-permute-start(bf16[2,2,2,120,240]{3,4,2,1,0:T(8,128)(2,1)} %copy.276), channel_id=1, source_target_pairs={{0,4},{4,0},{8,12},{12,8},{16,20},{20,16},{24,28},{28,24},{1,5},{5... | collective-permute-start | bytes 1382408 | tf_op jit(solution)/shard_map/ppermute | solution.py:44
  474.9 50.3 %collective-permute-start.15 = (bf16[2,2,2,120,240]{3,4,2,1,0:T(8,128)(2,1)}, bf16[2,2,2,120,240]{3,4,2,1,0:T(8,128)(2,1)}, u32[]{:S(2)}, u32[]{:S(2)}) collective-permute-start(bf16[2,2,2,120,240]{3,4,2,1,0:T(8,128)(2,1)} %copy.284), channel_id=1, source_target_pairs={{0,4},{4,0},{8,12},{12,8},{16,20},{20,16},{24,28},{28,24},{1,5},{5... | collective-permute-start | bytes 1382408 | tf_op jit(solution)/shard_map/ppermute | solution.py:44
  477.9 57.8 %collective-permute-start.3 = (bf16[1,640,512]{2,1,0:T(8,128)(2,1)}, bf16[1,640,512]{2,1,0:T(8,128)(2,1)}, u32[]{:S(2)}, u32[]{:S(2)}) collective-permute-start(bf16[1,640,512]{2,1,0:T(8,128)(2,1)} %add_convert_fusion.1), channel_id=1, source_target_pairs={{0,2},{1,3},{2,0},{3,1},{4,6},{5,7},{6,4},{7,5},{8,10},{9,11},{10,... | collective-permute-start | bytes 1966088 | tf_op jit(solution)/shard_map/ppermute | solution.py:44
  523.5 34.0 %collective-permute-start.29 = (bf16[2,2,2,2,120,640]{5,4,1,3,2,0:T(8,128)(2,1)}, bf16[2,2,2,2,120,640]{5,4,1,3,2,0:T(8,128)(2,1)}, u32[]{:S(2)}, u32[]{:S(2)}) collective-permute-start(bf16[2,2,2,2,120,640]{5,4,1,3,2,0:T(8,128)(2,1)} %copy.346), channel_id=1, source_target_pairs={{0,1},{1,0},{2,3},{3,2},{4,5},{5,4},{6,7},{7,6},{8,9},{9,8},{10,11... | collective-permute-start | bytes 7372808 | tf_op jit(solution)/shard_map/ppermute | solution.py:44
  523.5 37.9 %collective-permute-start.19 = (bf16[2,2,2,2,320,240]{5,4,1,3,2,0:T(8,128)(2,1)}, bf16[2,2,2,2,320,240]{5,4,1,3,2,0:T(8,128)(2,1)}, u32[]{:S(2)}, u32[]{:S(2)}) collective-permute-start(bf16[2,2,2,2,320,240]{5,4,1,3,2,0:T(8,128)(2,1)} %copy.343), channel_id=1, source_target_pairs={{0,1},{1,0},{2,3},{3,2},{4,5},{5,4},{6,7},{7,6},{8,9},{9,8},{10,11... | collective-permute-start | bytes 7372808 | tf_op jit(solution)/shard_map/ppermute | solution.py:44
  524.0 41.8 %collective-permute-start.24 = (bf16[2,2,2,2,320,240]{5,4,1,3,2,0:T(8,128)(2,1)}, bf16[2,2,2,2,320,240]{5,4,1,3,2,0:T(8,128)(2,1)}, u32[]{:S(2)}, u32[]{:S(2)}) collective-permute-start(bf16[2,2,2,2,320,240]{5,4,1,3,2,0:T(8,128)(2,1)} %copy.344), channel_id=1, source_target_pairs={{0,1},{1,0},{2,3},{3,2},{4,5},{5,4},{6,7},{7,6},{8,9},{9,8},{10,11... | collective-permute-start | bytes 7372808 | tf_op jit(solution)/shard_map/ppermute | solution.py:44
  533.7 20.8 %collective-permute-start.16 = (bf16[2,2,120,240]{2,3,1,0:T(8,128)(2,1)}, bf16[2,2,120,240]{2,3,1,0:T(8,128)(2,1)}, u32[]{:S(2)}, u32[]{:S(2)}) collective-permute-start(bf16[2,2,120,240]{2,3,1,0:T(8,128)(2,1)} %copy.286), channel_id=1, source_target_pairs={{0,2},{1,3},{2,0},{3,1},{4,6},{5,7},{6,4},{7,5},{8,10},{9,11},{10,... | collective-permute-start | bytes 691208 | tf_op jit(solution)/shard_map/ppermute | solution.py:44
  557.5 42.6 %collective-permute-start.13 = (bf16[120,240]{0,1:T(8,128)(2,1)S(1)}, bf16[120,240]{0,1:T(8,128)(2,1)S(1)}, u32[]{:S(2)}, u32[]{:S(2)}) collective-permute-start(bf16[120,240]{0,1:T(8,128)(2,1)S(1)} %fusion.130), channel_id=1, source_target_pairs={{0,16},{4,20},{8,24},{12,28},{16,0},{20,4},{24,8},{28,12},{1,17},{... | collective-permute-start | bytes 172808 | tf_op jit(solution)/shard_map/ppermute | solution.py:44
  561.4 54.8 %collective-permute-start.30 = (bf16[2,2,2,120,640]{4,3,2,1,0:T(8,128)(2,1)S(1)}, bf16[2,2,2,120,640]{4,3,2,1,0:T(8,128)(2,1)S(1)}, u32[]{:S(2)}, u32[]{:S(2)}) collective-permute-start(bf16[2,2,2,120,640]{4,3,2,1,0:T(8,128)(2,1)S(1)} %copy.324), channel_id=1, source_target_pairs={{0,2},{1,3},{2,0},{3,1},{4,6},{5,7},{6,4},{7,5},{8,10},{9,11},{10,... | collective-permute-start | bytes 3686408 | tf_op jit(solution)/shard_map/ppermute | solution.py:44
  565.0 47.5 %collective-permute-start.20 = (bf16[2,2,2,320,240]{4,3,2,1,0:T(8,128)(2,1)S(1)}, bf16[2,2,2,320,240]{4,3,2,1,0:T(8,128)(2,1)S(1)}, u32[]{:S(2)}, u32[]{:S(2)}) collective-permute-start(bf16[2,2,2,320,240]{4,3,2,1,0:T(8,128)(2,1)S(1)} %copy.296), channel_id=1, source_target_pairs={{0,4},{4,0},{8,12},{12,8},{16,20},{20,16},{24,28},{28,24},{1,5},{5... | collective-permute-start | bytes 3686408 | tf_op jit(solution)/shard_map/ppermute | solution.py:44
  565.8 33.4 %collective-permute-start.5 = (bf16[2,2,2,88,240]{4,3,2,1,0:T(8,128)(2,1)S(1)}, bf16[2,2,2,88,240]{4,3,2,1,0:T(8,128)(2,1)S(1)}, u32[]{:S(2)}, u32[]{:S(2)}) collective-permute-start(bf16[2,2,2,88,240]{4,3,2,1,0:T(8,128)(2,1)S(1)} %copy.268), channel_id=1, source_target_pairs={{0,2},{1,3},{2,0},{3,1},{4,6},{5,7},{6,4},{7,5},{8,10},{9,11},{10,... | collective-permute-start | bytes 1013768 | tf_op jit(solution)/shard_map/ppermute | solution.py:44
  568.5 58.8 %collective-permute-start.25 = (bf16[2,2,2,320,240]{4,3,2,1,0:T(8,128)(2,1)S(1)}, bf16[2,2,2,320,240]{4,3,2,1,0:T(8,128)(2,1)S(1)}, u32[]{:S(2)}, u32[]{:S(2)}) collective-permute-start(bf16[2,2,2,320,240]{4,3,2,1,0:T(8,128)(2,1)S(1)} %copy.310), channel_id=1, source_target_pairs={{0,2},{1,3},{2,0},{3,1},{4,6},{5,7},{6,4},{7,5},{8,10},{9,11},{10,... | collective-permute-start | bytes 3686408 | tf_op jit(solution)/shard_map/ppermute | solution.py:44
  614.4 25.2 %collective-permute-start.21 = (bf16[2,2,320,240]{3,2,0,1:T(8,128)(2,1)S(1)}, bf16[2,2,320,240]{3,2,0,1:T(8,128)(2,1)S(1)}, u32[]{:S(2)}, u32[]{:S(2)}) collective-permute-start(bf16[2,2,320,240]{3,2,0,1:T(8,128)(2,1)S(1)} %fusion.30), channel_id=1, source_target_pairs={{0,2},{1,3},{2,0},{3,1},{4,6},{5,7},{6,4},{7,5},{8,10},{9,11},{10,... | collective-permute-start | bytes 1843208 | tf_op jit(solution)/shard_map/ppermute | solution.py:44
  618.1 24.1 %collective-permute-start.31 = (bf16[2,2,120,640]{3,2,1,0:T(8,128)(2,1)S(1)}, bf16[2,2,120,640]{3,2,1,0:T(8,128)(2,1)S(1)}, u32[]{:S(2)}, u32[]{:S(2)}) collective-permute-start(bf16[2,2,120,640]{3,2,1,0:T(8,128)(2,1)S(1)} %copy.326), channel_id=1, source_target_pairs={{0,4},{4,0},{8,12},{12,8},{16,20},{20,16},{24,28},{28,24},{1,5},{5... | collective-permute-start | bytes 1843208 | tf_op jit(solution)/shard_map/ppermute | solution.py:44
  647.6 21.0 %collective-permute-start.27 = (bf16[2,320,240]{2,1,0:T(8,128)(2,1)}, bf16[2,320,240]{2,1,0:T(8,128)(2,1)}, u32[]{:S(2)}, u32[]{:S(2)}) collective-permute-start(bf16[2,320,240]{2,1,0:T(8,128)(2,1)} %fusion.36), channel_id=1, source_target_pairs={{0,8},{4,12},{8,0},{12,4},{16,24},{20,28},{24,16},{28,20},{1,9},{5... | collective-permute-start | bytes 921608 | tf_op jit(solution)/shard_map/ppermute | solution.py:44
  (96 other events, 849.9 us)
Sparse Core Ops, SparseCore 0:
  11.5 62.5 all-gather.10
  77.6 55.2 all-gather.12
  135.8 64.4 all-gather.16
  203.0 64.2 all-gather.14
  270.0 63.2 all-gather.18
